TPU v7x, 32 devices: a whole 2x2x4 slice. The times are simulated.
32 devices in a mesh: gy: 8 (over z, x), gz: 4 (over y, core).
Axes of the slice: x: 2, y: 2, z: 4, core: 2. Of those that a mesh axis runs over, the one named last changes fastest.
Arguments:
- species_field: float32 [256, 256, 256], P('gy', 'gz'), may hold values from -10 to 10
- reaction_source: float32 [256, 256, 256], P('gy', 'gz'), may hold values from -1500 to 1500
- interface_mask: int32 [256, 256, 256], P('gy', 'gz'), may hold values 0 or 1
- phase_labels: int32 [256, 256, 256], P('gy', 'gz'), may hold values from 0 to 3
- phase_diffusivity: float32 [4], replicated, may hold values from 1 to 16
Outputs:
- updated_field: float32 [256, 256, 256], P('gy', 'gz')
All inputs are finite; a program needn't handle non-finite values. No bound on the sum of `interface_mask` on one device may be relied on, other than what follows from the above.
Results may differ from a plain program's by a relative error of at most 0.0003.
Values sent between devices are 32-bit elements; how exact they have to be, the bound alone decides.
A program may use at most 128 MiB of HBM per device.

v0:
```python
import functools

import jax
import jax.numpy as jnp
from jax import lax
from jax.experimental import pallas as pl
from jax.experimental.pallas import tpu as pltpu
from jax.sharding import PartitionSpec as P

NU = 400
LANES = 128
MESH = pl.DeviceIdType.MESH


def recip(value):
    return pl.reciprocal(value, approx=False)


def eliminate(slack, rate):
    excess = rate + slack
    ratio = recip(1.0 + excess)
    return excess * ratio, ratio


def kernel(
    ny, nz, ly, lz, lx, phases,
    diff, u_hbm, s_hbm, m_hbm, l_hbm, out_hbm,
    u_v, s_v, m_v, l_v, g_v, cy, cz, lapz, rt, cx, r2, rz, out_v,
    zh_send, zh_recv, ye_send, ye_recv, yp_send, yp_recv, ya_send, ya_recv, ze, zp,
    ychain, zchain,
    loc_sem, out_sem, hy_s, hy_r, hz_s, hz_r, ye_s, ye_r, yp_s, yp_r, ya_s, ya_r,
    ze_s, ze_r, zp_s, zp_r,
):
    halves = lx // LANES
    rows = ly * lz
    blocks = rows // LANES
    per_block = LANES // lz
    rp = lz // ny
    half_x = lx // 2
    me_y = lax.axis_index("gy")
    me_z = lax.axis_index("gz")
    up_y, down_y = lax.rem(me_y + 1, ny), lax.rem(me_y + ny - 1, ny)
    up_z, down_z = lax.rem(me_z + 1, nz), lax.rem(me_z + nz - 1, nz)

    loads = []
    for index, (src, dst) in enumerate(((l_hbm, l_v), (u_hbm, u_v), (s_hbm, s_v), (m_hbm, m_v))):
        pair = []
        for h in range(halves):
            target = dst[h].at[pl.ds(1, ly)] if dst is u_v else dst[h]
            copy = pltpu.make_async_copy(
                src.at[:, :, pl.ds(h * LANES, LANES)], target, loc_sem.at[index, h]
            )
            copy.start()
            pair.append(copy)
        loads.append(pair)

    barrier = pltpu.get_barrier_semaphore()

    def greet(axis, me, n):
        def one(o, _):
            pl.semaphore_signal(
                barrier, inc=1, device_id={axis: lax.rem(me + o, n)}, device_id_type=MESH
            )
            return 0
        lax.fori_loop(1, n, one, 0)

    greet("gy", me_y, ny)
    greet("gz", me_z, nz)
    pl.semaphore_wait(barrier, ny + nz - 2)

    halo_y = []
    for h in range(halves):
        cols = pl.ds(h * LANES, LANES)
        for d, (row, place, peer) in enumerate(((ly - 1, 0, up_y), (0, ly + 1, down_y))):
            copy = pltpu.make_async_remote_copy(
                src_ref=u_hbm.at[row, :, cols], dst_ref=u_v[h].at[place],
                send_sem=hy_s.at[h, d], recv_sem=hy_r.at[h, d],
                device_id={"gy": peer}, device_id_type=MESH,
            )
            copy.start()
            halo_y.append(copy)

    for h in range(halves):
        loads[1][h].wait()
        for d, z in ((0, lz - 1), (1, 0)):
            def pick(y, _):
                zh_send[d, h, pl.ds(y, 1), :] = u_v[h][y + 1, pl.ds(z, 1), :]
                return 0
            lax.fori_loop(0, ly, pick, 0, unroll=8)
    halo_z = []
    for d, peer in ((0, up_z), (1, down_z)):
        copy = pltpu.make_async_remote_copy(
            src_ref=zh_send.at[d], dst_ref=zh_recv.at[d],
            send_sem=hz_s.at[d], recv_sem=hz_r.at[d],
            device_id={"gz": peer}, device_id_type=MESH,
        )
        copy.start()
        halo_z.append(copy)

    def spread(axis, me, n, source, target, send, recv, start):
        def one(o, _):
            peer = lax.rem(me + o, n)
            if start:
                pltpu.make_async_remote_copy(
                    src_ref=source(peer), dst_ref=target(me),
                    send_sem=send(peer), recv_sem=recv(me),
                    device_id={axis: peer}, device_id_type=MESH,
                ).start()
            else:
                copy = pltpu.make_async_remote_copy(
                    src_ref=source(peer), dst_ref=target(peer),
                    send_sem=send(peer), recv_sem=recv(peer),
                    device_id={axis: peer}, device_id_type=MESH,
                )
                copy.wait_send()
                copy.wait_recv()
            return 0
        lax.fori_loop(1, n, one, 0)

    def ye_do(start):
        spread("gy", me_y, ny, lambda p: ye_send.at[p], lambda p: ye_recv.at[p],
               lambda p: ye_s.at[p], lambda p: ye_r.at[p], start)

    def yp_do(h, start):
        spread("gy", me_y, ny, lambda p: yp_send.at[h, p], lambda p: yp_recv.at[h, p],
               lambda p: yp_s.at[h, p], lambda p: yp_r.at[h, p], start)

    def ya_do(h, start):
        spread("gy", me_y, ny, lambda p: ya_send.at[h, p], lambda p: ya_recv.at[h, p],
               lambda p: ya_s.at[h, p], lambda p: ya_r.at[h, p], start)

    def ze_do(start):
        spread("gz", me_z, nz, lambda p: ze.at[me_z], lambda p: ze.at[p],
               lambda p: ze_s.at[p], lambda p: ze_r.at[p], start)

    def zp_do(h, start):
        spread("gz", me_z, nz, lambda p: zp.at[h, me_z], lambda p: zp.at[h, p],
               lambda p: zp_s.at[h, p], lambda p: zp_r.at[h, p], start)

    inv = [recip(0.5 * NU * jnp.full((8, LANES), diff[k], jnp.float32))[:1] for k in range(phases)]
    plane = (lz, LANES)
    ones, zeros = jnp.ones(plane, jnp.float32), jnp.zeros(plane, jnp.float32)
    for h in range(halves):
        loads[0][h].wait()

        def matrix_y(y, carry):
            slack, prod, low, _ = carry
            at = pl.ds(pl.multiple_of(y * lz, lz), lz)
            label = l_v[h][y]
            rate = jnp.broadcast_to(inv[0], plane)
            for k in range(1, phases):
                rate = jnp.where(label == k, inv[k], rate)
            g_v[h][at, :] = rate
            slack, ratio = eliminate(slack, rate)
            cy[h][at, :] = ratio
            later = prod * ratio
            return slack, later, low + prod * later, ratio

        _, prod, low, last = lax.fori_loop(0, ly, matrix_y, (ones, ones, zeros, zeros))
        for j in range(ny):
            part = slice(rp * j, rp * (j + 1))
            ye_send[j, h, 0] = low[part]
            ye_send[j, h, 1] = prod[part]
            ye_send[j, h, 2] = last[part]
    ye_recv[me_y] = ye_send[me_y]
    ye_do(True)

    slab = (ly, LANES)
    zones, zzeros = jnp.ones(slab, jnp.float32), jnp.zeros(slab, jnp.float32)
    for h in range(halves):
        def matrix_z(z, carry):
            slack, prod, low, _ = carry
            rate = g_v[h][pl.ds(z, ly, stride=lz), :]
            slack, ratio = eliminate(slack, rate)
            cz[h][z] = ratio
            later = prod * ratio
            return slack, later, low + prod * later, ratio

        _, prod, low, last = lax.fori_loop(
            0, lz, matrix_z, (zones, zzeros + 1.0, zzeros, zzeros), unroll=2
        )
        ze[me_z, h, 0] = low
        ze[me_z, h, 1] = prod
        ze[me_z, h, 2] = last
    ze_do(True)

    for h in range(halves):
        def turn_g(b, _):
            block = g_v[h][pl.ds(pl.multiple_of(b * LANES, LANES), LANES), :]
            cx[pl.ds(h * LANES * blocks + b, LANES, stride=blocks), :] = block.T
            return 0
        lax.fori_loop(0, blocks, turn_g, 0, unroll=2)

    def at_x(i):
        return pl.ds(pl.multiple_of(i * blocks, blocks), blocks)

    lines = (blocks, LANES)
    lone, lzero = jnp.ones(lines, jnp.float32), jnp.zeros(lines, jnp.float32)

    def matrix_x(i, carry):
        one, two = carry
        one, ratio = eliminate(one, cx[at_x(i), :])
        cx[at_x(i), :] = ratio
        two, ratio = eliminate(two, cx[at_x(lx - 1 - i), :])
        cx[at_x(lx - 1 - i), :] = ratio
        return one, two

    slack_one, slack_two = lax.fori_loop(0, half_x, matrix_x, (lone, lone), unroll=4)
    middle = recip(slack_one + slack_two - slack_one * slack_two)

    for copy in halo_y + halo_z:
        copy.wait()
    for h in range(halves):
        loads[2][h].wait()
        loads[3][h].wait()

        @pl.when(me_y == 0)
        def _():
            u_v[h][0] = zeros

        @pl.when(me_y == ny - 1)
        def _():
            u_v[h][ly + 1] = zeros

        @pl.when(me_z == 0)
        def _():
            zh_recv[0, h] = zzeros

        @pl.when(me_z == nz - 1)
        def _():
            zh_recv[1, h] = zzeros

    sub = lax.broadcasted_iota(jnp.int32, plane, 0)
    lane = lax.broadcasted_iota(jnp.int32, plane, 1)

    def right_x(b, _):
        done = [[] for _ in range(halves)]
        for k in range(per_block):
            y = b * per_block + k
            at = pl.ds(pl.multiple_of(y * lz, lz), lz)
            mids = [u_v[h][y + 1] for h in range(halves)]
            ups = [pltpu.roll(m, LANES - 1, 1) for m in mids]
            downs = [pltpu.roll(m, 1, 1) for m in mids]
            for h in range(halves):
                mid = mids[h]
                after = jnp.where(lane == LANES - 1, ups[h + 1] if h + 1 < halves else 0.0, ups[h])
                before = jnp.where(lane == 0, downs[h - 1] if h else 0.0, downs[h])
                twice = 2.0 * mid
                lap_x = after + before - twice
                lap_y = u_v[h][y] + u_v[h][y + 2] - twice
                below = jnp.where(sub == 0, zh_recv[0, h, pl.ds(y, 1), :], pltpu.roll(mid, 1, 0))
                above = jnp.where(
                    sub == lz - 1, zh_recv[1, h, pl.ds(y, 1), :], pltpu.roll(mid, lz - 1, 0)
                )
                lap_z = below + above - twice
                lapz[h][at, :] = lap_z
                source = m_v[h][y].astype(jnp.float32) * s_v[h][y]
                value = g_v[h][at, :] * (mid + source) + (lap_x + 2.0 * (lap_y + lap_z))
                done[h].append(value)
        for h in range(halves):
            block = jnp.concatenate(done[h], 0)
            rt[pl.ds(h * LANES * blocks + b, LANES, stride=blocks), :] = block.T
        return 0

    lax.fori_loop(0, blocks, right_x, 0)

    def forward_x(i, carry):
        one, two = carry
        low_at, high_at = at_x(i), at_x(lx - 1 - i)
        one = (rt[low_at, :] + one) * cx[low_at, :]
        rt[low_at, :] = one
        two = (rt[high_at, :] + two) * cx[high_at, :]
        rt[high_at, :] = two
        return one, two

    one, two = lax.fori_loop(0, half_x, forward_x, (lzero, lzero), unroll=8)
    low_mid, high_mid = at_x(half_x - 1), at_x(half_x)
    first = (one + cx[low_mid, :] * two) * middle
    second = (two + cx[high_mid, :] * one) * middle
    rt[low_mid, :] = first
    rt[high_mid, :] = second

    def backward_x(i, carry):
        one, two = carry
        low_at, high_at = at_x(half_x - 1 - i), at_x(half_x + i)
        one = rt[low_at, :] + cx[low_at, :] * one
        rt[low_at, :] = one
        two = rt[high_at, :] + cx[high_at, :] * two
        rt[high_at, :] = two
        return one, two

    lax.fori_loop(1, half_x, backward_x, (first, second), unroll=8)

    for h in range(halves):
        def local_y(b, carry):
            value, prod, head = carry
            block = rt[pl.ds(h * LANES * blocks + b, LANES, stride=blocks), :].T
            for k in range(per_block):
                y = b * per_block + k
                at = pl.ds(pl.multiple_of(y * lz, lz), lz)
                lap_y = u_v[h][y] + u_v[h][y + 2] - 2.0 * u_v[h][y + 1]
                right = g_v[h][at, :] * block[k * lz:(k + 1) * lz] - lap_y
                r2[h][at, :] = right
                ratio = cy[h][at, :]
                value = (right + value) * ratio
                head = head + value * prod
                prod = prod * ratio
            return value, prod, head

        value, _, head = lax.fori_loop(0, blocks, local_y, (zeros, ones, zeros))
        for j in range(ny):
            part = slice(rp * j, rp * (j + 1))
            yp_send[h, j, 0] = head[part]
            yp_send[h, j, 1] = value[part]
        yp_recv[h, me_y] = yp_send[h, me_y]
        yp_do(h, True)

    def chain(n, coef, plain, keep, answer, shape):
        none = jnp.zeros(shape, jnp.float32)

        def forward(k, carry):
            offset, slope = carry
            low, cross, high = coef(k, 0), coef(k, 1), coef(k, 2)
            pivot = recip(1.0 - low * slope)
            head = pivot * (plain(k, 0) + low * offset)
            keep[k, 0] = offset
            keep[k, 1] = slope
            keep[k, 2] = head
            keep[k, 3] = pivot * cross
            return (
                plain(k, 1) + cross * (offset + slope * head),
                high + cross * cross * slope * pivot,
            )

        lax.fori_loop(0, n, forward, (none, none))

        def backward(i, after):
            k = n - 1 - i
            head = keep[k, 2] + keep[k, 3] * after
            answer(k, keep[k, 0] + keep[k, 1] * head, after)
            return head

        lax.fori_loop(0, n, backward, none)

    ye_do(False)
    for h in range(halves):
        yp_do(h, False)

        def answer_y(k, left, right):
            ya_send[h, k, 0] = left
            ya_send[h, k, 1] = right

        chain(ny, lambda k, c: ye_recv[k, h, c], lambda k, c: yp_recv[h, k, c],
              ychain, answer_y, (rp, LANES))
        ya_recv[h, me_y] = ya_send[h, me_y]
        ya_do(h, True)

    for h in range(halves):
        ya_do(h, False)
        left = jnp.concatenate([ya_recv[h, j, 0] for j in range(ny)], 0)
        right = jnp.concatenate([ya_recv[h, j, 1] for j in range(ny)], 0)

        def forward_y(y, value):
            at = pl.ds(pl.multiple_of(y * lz, lz), lz)
            value = (r2[h][at, :] + value) * cy[h][at, :]
            r2[h][at, :] = value
            return value

        lax.fori_loop(0, ly, forward_y, left, unroll=2)

        def backward_y(i, value):
            y = ly - 1 - i
            at = pl.ds(pl.multiple_of(y * lz, lz), lz)
            value = r2[h][at, :] + cy[h][at, :] * value
            rz[h][pl.ds(y, lz, stride=ly), :] = g_v[h][at, :] * value - lapz[h][at, :]
            return value

        lax.fori_loop(0, ly, backward_y, right, unroll=2)

        def local_z(z, carry):
            value, prod, head = carry
            ratio = cz[h][z]
            value = (rz[h][pl.ds(pl.multiple_of(z * ly, ly), ly), :] + value) * ratio
            return value, prod * ratio, head + value * prod

        value, _, head = lax.fori_loop(0, lz, local_z, (zzeros, zones, zzeros), unroll=4)
        zp[h, me_z, 0] = head
        zp[h, me_z, 1] = value
        zp_do(h, True)

    ze_do(False)
    for h in range(halves):
        zp_do(h, False)

        def answer_z(k, left, right):
            zchain[k, 4] = left
            zchain[k, 5] = right

        chain(nz, lambda k, c: ze[k, h, c], lambda k, c: zp[h, k, c], zchain, answer_z, slab)
        left, right = zchain[me_z, 4], zchain[me_z, 5]

        def forward_z(z, value):
            at = pl.ds(pl.multiple_of(z * ly, ly), ly)
            value = (rz[h][at, :] + value) * cz[h][z]
            rz[h][at, :] = value
            return value

        lax.fori_loop(0, lz, forward_z, left, unroll=4)

        def backward_z(i, value):
            z = lz - 1 - i
            value = rz[h][pl.ds(pl.multiple_of(z * ly, ly), ly), :] + cz[h][z] * value
            out_v[h][pl.ds(z, ly, stride=lz), :] = value
            return value

        lax.fori_loop(0, lz, backward_z, right, unroll=4)

        def send_out(y, _):
            pltpu.make_async_copy(
                out_v[h].at[pl.ds(pl.multiple_of(y * lz, lz), lz), :],
                out_hbm.at[y, :, pl.ds(h * LANES, LANES)], out_sem.at[h, y],
            ).start()
            return 0

        lax.fori_loop(0, ly, send_out, 0)

    for h in range(halves):
        def wait_out(y, _):
            pltpu.make_async_copy(
                out_v[h].at[pl.ds(pl.multiple_of(y * lz, lz), lz), :],
                out_hbm.at[y, :, pl.ds(h * LANES, LANES)], out_sem.at[h, y],
            ).wait()
            return 0

        lax.fori_loop(0, ly, wait_out, 0)


def body(ny, nz, species_field, reaction_source, interface_mask, phase_labels, phase_diffusivity):
    ly, lz, lx = species_field.shape
    halves = lx // LANES
    rows = ly * lz
    blocks = rows // LANES
    rp = lz // ny
    f32 = jnp.float32

    def vm(*shape, dtype=f32):
        return pltpu.VMEM(shape, dtype)

    def pair(*shape, dtype=f32):
        return [vm(*shape, dtype=dtype) for _ in range(halves)]

    def sems(*shape):
        return pltpu.SemaphoreType.DMA(shape)

    scratch = [
        pair(ly + 2, lz, LANES), pair(ly, lz, LANES),
        pair(ly, lz, LANES, dtype=jnp.int32), pair(ly, lz, LANES, dtype=jnp.int32),
        pair(rows, LANES), pair(rows, LANES), pair(lz, ly, LANES), pair(rows, LANES),
        vm(lx * blocks, LANES), vm(lx * blocks, LANES),
        pair(rows, LANES), pair(rows, LANES), pair(rows, LANES),
        vm(2, halves, ly, LANES), vm(2, halves, ly, LANES),
        vm(ny, halves, 3, rp, LANES), vm(ny, halves, 3, rp, LANES),
        vm(halves, ny, 2, rp, LANES), vm(halves, ny, 2, rp, LANES),
        vm(halves, ny, 2, rp, LANES), vm(halves, ny, 2, rp, LANES),
        vm(nz, halves, 3, ly, LANES), vm(halves, nz, 2, ly, LANES),
        vm(ny, 4, rp, LANES), vm(nz, 6, ly, LANES),
        sems(4, halves), sems(halves, ly),
        sems(halves, 2), sems(halves, 2), sems(2), sems(2),
        sems(ny), sems(ny), sems(halves, ny), sems(halves, ny), sems(halves, ny), sems(halves, ny),
        sems(nz), sems(nz), sems(halves, nz), sems(halves, nz),
    ]
    anywhere = pl.BlockSpec(memory_space=pl.ANY)
    return pl.pallas_call(
        functools.partial(kernel, ny, nz, ly, lz, lx, phase_diffusivity.shape[0]),
        out_shape=jax.ShapeDtypeStruct(species_field.shape, f32),
        in_specs=[pl.BlockSpec(memory_space=pltpu.SMEM)] + [anywhere] * 4,
        out_specs=anywhere,
        scratch_shapes=scratch,
        compiler_params=pltpu.CompilerParams(
            collective_id=0, has_side_effects=True, vmem_limit_bytes=56 * 1024 * 1024
        ),
    )(phase_diffusivity, species_field, reaction_source, interface_mask, phase_labels)


def solution(mesh):
    spec = P("gy", "gz", None)
    return jax.shard_map(
        functools.partial(body, mesh.shape["gy"], mesh.shape["gz"]),
        mesh=mesh, in_specs=(spec,) * 4 + (P(),), out_specs=spec, check_vma=False,
    )
```

profile of v0, /device:TPU:0, one launch (start us, length us, event | category | flops | bytes accessed | tf_op | source)
XLA Modules:
  0.0 45.6 jit_solution(7568594590868532388)
XLA Ops:
  0.0 42.5 %shard_map.55 = f32[32,64,256]{2,1,0:T(8,128)} custom-call(f32[4]{0:T(128)} %diff.1, f32[32,64,256]{2,1,0:T(8,128)} %u_hbm.1, f32[32,64,256]{2,1,0:T(8,128)} %s_hbm.1, s32[32,64,256]{2,1,0:T(8,128)} %m_hbm.1, s32[32,64,256]{2,1,0:T(8,128)} %l_hbm.1), custom_call_target="tpu_custom_call" | custom-call | tf_op jit(solution)/shard_map/pallas_call | solution.py:473
  42.5 3.1 %copy.7 = f32[32,64,256]{2,1,0:T(8,128)} copy(f32[32,64,256]{2,1,0:T(8,128)} %shard_map.55) | data formatting | bytes 4194304
where the time goes:
time: 45.8 us; the launch traced here: 45.6 us
  Pallas kernels  42.5 us (93%)
  local copies, waits for them, and re-layouts  3.13 us (7%)
    pallas_call x1, Pallas kernels, body(): pl.pallas_call(functools.partial(kernel, ny, nz, ly, lz, lx, phase_diffus...  42.5 us
    unnamed x1, local copies, waits for them, and re-layouts  3.13 us

commit v1 on v0

--- a/solution.py
+++ b/solution.py
@@ -24,11 +24,11 @@
 
 def kernel(
     ny, nz, ly, lz, lx, phases,
-    diff, u_hbm, s_hbm, m_hbm, l_hbm, out_hbm,
-    u_v, s_v, m_v, l_v, g_v, cy, cz, lapz, rt, cx, r2, rz, out_v,
+    diff, u_hbm, s_hbm, m_hbm, l_hbm, out,
+    u_v, s_v, m_v, l_v, g_v, cy, cz, lapz, rt, cx, r2, rz,
     zh_send, zh_recv, ye_send, ye_recv, yp_send, yp_recv, ya_send, ya_recv, ze, zp,
     ychain, zchain,
-    loc_sem, out_sem, hy_s, hy_r, hz_s, hz_r, ye_s, ye_r, yp_s, yp_r, ya_s, ya_r,
+    loc_sem, hy_s, hy_r, hz_s, hz_r, ye_s, ye_r, yp_s, yp_r, ya_s, ya_r,
     ze_s, ze_r, zp_s, zp_r,
 ):
     halves = lx // LANES
@@ -37,6 +37,7 @@
     per_block = LANES // lz
     rp = lz // ny
     half_x = lx // 2
+    pitch_x, pitch_z = blocks + 1, ly + 1
     me_y = lax.axis_index("gy")
     me_z = lax.axis_index("gz")
     up_y, down_y = lax.rem(me_y + 1, ny), lax.rem(me_y + ny - 1, ny)
@@ -138,6 +139,8 @@
                lambda p: zp_s.at[h, p], lambda p: zp_r.at[h, p], start)
 
     inv = [recip(0.5 * NU * jnp.full((8, LANES), diff[k], jnp.float32))[:1] for k in range(phases)]
+    slab = (ly, LANES)
+    zones, zzeros = jnp.ones(slab, jnp.float32), jnp.zeros(slab, jnp.float32)
     plane = (lz, LANES)
     ones, zeros = jnp.ones(plane, jnp.float32), jnp.zeros(plane, jnp.float32)
     for h in range(halves):
@@ -151,6 +154,7 @@
             for k in range(1, phases):
                 rate = jnp.where(label == k, inv[k], rate)
             g_v[h][at, :] = rate
+            rz[h][pl.ds(y, lz, stride=pitch_z), :] = rate
             slack, ratio = eliminate(slack, rate)
             cy[h][at, :] = ratio
             later = prod * ratio
@@ -165,34 +169,15 @@
     ye_recv[me_y] = ye_send[me_y]
     ye_do(True)
 
-    slab = (ly, LANES)
-    zones, zzeros = jnp.ones(slab, jnp.float32), jnp.zeros(slab, jnp.float32)
-    for h in range(halves):
-        def matrix_z(z, carry):
-            slack, prod, low, _ = carry
-            rate = g_v[h][pl.ds(z, ly, stride=lz), :]
-            slack, ratio = eliminate(slack, rate)
-            cz[h][z] = ratio
-            later = prod * ratio
-            return slack, later, low + prod * later, ratio
-
-        _, prod, low, last = lax.fori_loop(
-            0, lz, matrix_z, (zones, zzeros + 1.0, zzeros, zzeros), unroll=2
-        )
-        ze[me_z, h, 0] = low
-        ze[me_z, h, 1] = prod
-        ze[me_z, h, 2] = last
-    ze_do(True)
-
     for h in range(halves):
         def turn_g(b, _):
             block = g_v[h][pl.ds(pl.multiple_of(b * LANES, LANES), LANES), :]
-            cx[pl.ds(h * LANES * blocks + b, LANES, stride=blocks), :] = block.T
+            cx[pl.ds(h * LANES * pitch_x + b, LANES, stride=pitch_x), :] = block.T
             return 0
         lax.fori_loop(0, blocks, turn_g, 0, unroll=2)
 
     def at_x(i):
-        return pl.ds(pl.multiple_of(i * blocks, blocks), blocks)
+        return pl.ds(i * pitch_x, blocks)
 
     lines = (blocks, LANES)
     lone, lzero = jnp.ones(lines, jnp.float32), jnp.zeros(lines, jnp.float32)
@@ -259,7 +244,7 @@
                 done[h].append(value)
         for h in range(halves):
             block = jnp.concatenate(done[h], 0)
-            rt[pl.ds(h * LANES * blocks + b, LANES, stride=blocks), :] = block.T
+            rt[pl.ds(h * LANES * pitch_x + b, LANES, stride=pitch_x), :] = block.T
         return 0
 
     lax.fori_loop(0, blocks, right_x, 0)
@@ -294,7 +279,7 @@
     for h in range(halves):
         def local_y(b, carry):
             value, prod, head = carry
-            block = rt[pl.ds(h * LANES * blocks + b, LANES, stride=blocks), :].T
+            block = rt[pl.ds(h * LANES * pitch_x + b, LANES, stride=pitch_x), :].T
             for k in range(per_block):
                 y = b * per_block + k
                 at = pl.ds(pl.multiple_of(y * lz, lz), lz)
@@ -315,34 +300,56 @@
         yp_recv[h, me_y] = yp_send[h, me_y]
         yp_do(h, True)
 
+    def pivots(n, coef, keep, shape):
+        def one(k, slope):
+            low, cross = coef(k, 0), coef(k, 1)
+            pivot = recip(1.0 - low * slope)
+            keep[k, 0] = slope
+            keep[k, 1] = pivot
+            keep[k, 2] = pivot * cross
+            return coef(k, 2) + cross * cross * slope * pivot
+
+        lax.fori_loop(0, n, one, jnp.zeros(shape, jnp.float32))
+
     def chain(n, coef, plain, keep, answer, shape):
         none = jnp.zeros(shape, jnp.float32)
 
-        def forward(k, carry):
-            offset, slope = carry
-            low, cross, high = coef(k, 0), coef(k, 1), coef(k, 2)
-            pivot = recip(1.0 - low * slope)
-            head = pivot * (plain(k, 0) + low * offset)
-            keep[k, 0] = offset
-            keep[k, 1] = slope
-            keep[k, 2] = head
-            keep[k, 3] = pivot * cross
-            return (
-                plain(k, 1) + cross * (offset + slope * head),
-                high + cross * cross * slope * pivot,
-            )
-
-        lax.fori_loop(0, n, forward, (none, none))
+        def forward(k, offset):
+            head = keep[k, 1] * (plain(k, 0) + coef(k, 0) * offset)
+            keep[k, 3] = offset
+            keep[k, 4] = head
+            return plain(k, 1) + coef(k, 1) * (offset + keep[k, 0] * head)
+
+        lax.fori_loop(0, n, forward, none)
 
         def backward(i, after):
             k = n - 1 - i
-            head = keep[k, 2] + keep[k, 3] * after
-            answer(k, keep[k, 0] + keep[k, 1] * head, after)
+            head = keep[k, 4] + keep[k, 2] * after
+            answer(k, keep[k, 3] + keep[k, 0] * head, after)
             return head
 
         lax.fori_loop(0, n, backward, none)
 
+    for h in range(halves):
+        def matrix_z(z, carry):
+            slack, prod, low, _ = carry
+            rate = rz[h][pl.ds(z * pitch_z, ly), :]
+            slack, ratio = eliminate(slack, rate)
+            cz[h][z] = ratio
+            later = prod * ratio
+            return slack, later, low + prod * later, ratio
+
+        _, prod, low, last = lax.fori_loop(
+            0, lz, matrix_z, (zones, zzeros + 1.0, zzeros, zzeros), unroll=2
+        )
+        ze[me_z, h, 0] = low
+        ze[me_z, h, 1] = prod
+        ze[me_z, h, 2] = last
+    ze_do(True)
+
     ye_do(False)
+    for h in range(halves):
+        pivots(ny, lambda k, c: ye_recv[k, h, c], ychain.at[h], (rp, LANES))
     for h in range(halves):
         yp_do(h, False)
 
@@ -351,9 +358,13 @@
             ya_send[h, k, 1] = right
 
         chain(ny, lambda k, c: ye_recv[k, h, c], lambda k, c: yp_recv[h, k, c],
-              ychain, answer_y, (rp, LANES))
+              ychain.at[h], answer_y, (rp, LANES))
         ya_recv[h, me_y] = ya_send[h, me_y]
         ya_do(h, True)
+
+    ze_do(False)
+    for h in range(halves):
+        pivots(nz, lambda k, c: ze[k, h, c], zchain.at[h], slab)
 
     for h in range(halves):
         ya_do(h, False)
@@ -372,7 +383,7 @@
             y = ly - 1 - i
             at = pl.ds(pl.multiple_of(y * lz, lz), lz)
             value = r2[h][at, :] + cy[h][at, :] * value
-            rz[h][pl.ds(y, lz, stride=ly), :] = g_v[h][at, :] * value - lapz[h][at, :]
+            rz[h][pl.ds(y, lz, stride=pitch_z), :] = g_v[h][at, :] * value - lapz[h][at, :]
             return value
 
         lax.fori_loop(0, ly, backward_y, right, unroll=2)
@@ -380,7 +391,7 @@
         def local_z(z, carry):
             value, prod, head = carry
             ratio = cz[h][z]
-            value = (rz[h][pl.ds(pl.multiple_of(z * ly, ly), ly), :] + value) * ratio
+            value = (rz[h][pl.ds(z * pitch_z, ly), :] + value) * ratio
             return value, prod * ratio, head + value * prod
 
         value, _, head = lax.fori_loop(0, lz, local_z, (zzeros, zones, zzeros), unroll=4)
@@ -388,19 +399,19 @@
         zp[h, me_z, 1] = value
         zp_do(h, True)
 
-    ze_do(False)
     for h in range(halves):
         zp_do(h, False)
 
         def answer_z(k, left, right):
-            zchain[k, 4] = left
-            zchain[k, 5] = right
-
-        chain(nz, lambda k, c: ze[k, h, c], lambda k, c: zp[h, k, c], zchain, answer_z, slab)
-        left, right = zchain[me_z, 4], zchain[me_z, 5]
+            zchain[h, k, 5] = left
+            zchain[h, k, 6] = right
+
+        chain(nz, lambda k, c: ze[k, h, c], lambda k, c: zp[h, k, c],
+              zchain.at[h], answer_z, slab)
+        left, right = zchain[h, me_z, 5], zchain[h, me_z, 6]
 
         def forward_z(z, value):
-            at = pl.ds(pl.multiple_of(z * ly, ly), ly)
+            at = pl.ds(z * pitch_z, ly)
             value = (rz[h][at, :] + value) * cz[h][z]
             rz[h][at, :] = value
             return value
@@ -409,30 +420,17 @@
 
         def backward_z(i, value):
             z = lz - 1 - i
-            value = rz[h][pl.ds(pl.multiple_of(z * ly, ly), ly), :] + cz[h][z] * value
-            out_v[h][pl.ds(z, ly, stride=lz), :] = value
+            value = rz[h][pl.ds(z * pitch_z, ly), :] + cz[h][z] * value
+            rz[h][pl.ds(z * pitch_z, ly), :] = value
             return value
 
         lax.fori_loop(0, lz, backward_z, right, unroll=4)
 
-        def send_out(y, _):
-            pltpu.make_async_copy(
-                out_v[h].at[pl.ds(pl.multiple_of(y * lz, lz), lz), :],
-                out_hbm.at[y, :, pl.ds(h * LANES, LANES)], out_sem.at[h, y],
-            ).start()
+        def turn_out(y, _):
+            out[y, :, pl.ds(h * LANES, LANES)] = rz[h][pl.ds(y, lz, stride=pitch_z), :]
             return 0
 
-        lax.fori_loop(0, ly, send_out, 0)
-
-    for h in range(halves):
-        def wait_out(y, _):
-            pltpu.make_async_copy(
-                out_v[h].at[pl.ds(pl.multiple_of(y * lz, lz), lz), :],
-                out_hbm.at[y, :, pl.ds(h * LANES, LANES)], out_sem.at[h, y],
-            ).wait()
-            return 0
-
-        lax.fori_loop(0, ly, wait_out, 0)
+        lax.fori_loop(0, ly, turn_out, 0, unroll=4)
 
 
 def body(ny, nz, species_field, reaction_source, interface_mask, phase_labels, phase_diffusivity):
@@ -456,15 +454,15 @@
         pair(ly + 2, lz, LANES), pair(ly, lz, LANES),
         pair(ly, lz, LANES, dtype=jnp.int32), pair(ly, lz, LANES, dtype=jnp.int32),
         pair(rows, LANES), pair(rows, LANES), pair(lz, ly, LANES), pair(rows, LANES),
-        vm(lx * blocks, LANES), vm(lx * blocks, LANES),
-        pair(rows, LANES), pair(rows, LANES), pair(rows, LANES),
+        vm(lx * (blocks + 1), LANES), vm(lx * (blocks + 1), LANES),
+        pair(rows, LANES), pair(lz * (ly + 1), LANES),
         vm(2, halves, ly, LANES), vm(2, halves, ly, LANES),
         vm(ny, halves, 3, rp, LANES), vm(ny, halves, 3, rp, LANES),
         vm(halves, ny, 2, rp, LANES), vm(halves, ny, 2, rp, LANES),
         vm(halves, ny, 2, rp, LANES), vm(halves, ny, 2, rp, LANES),
         vm(nz, halves, 3, ly, LANES), vm(halves, nz, 2, ly, LANES),
-        vm(ny, 4, rp, LANES), vm(nz, 6, ly, LANES),
-        sems(4, halves), sems(halves, ly),
+        vm(halves, ny, 5, rp, LANES), vm(halves, nz, 7, ly, LANES),
+        sems(4, halves),
         sems(halves, 2), sems(halves, 2), sems(2), sems(2),
         sems(ny), sems(ny), sems(halves, ny), sems(halves, ny), sems(halves, ny), sems(halves, ny),
         sems(nz), sems(nz), sems(halves, nz), sems(halves, nz),
@@ -472,9 +470,9 @@
     anywhere = pl.BlockSpec(memory_space=pl.ANY)
     return pl.pallas_call(
         functools.partial(kernel, ny, nz, ly, lz, lx, phase_diffusivity.shape[0]),
-        out_shape=jax.ShapeDtypeStruct(species_field.shape, f32),
+        out_shape=pltpu.VMEM(species_field.shape, f32),
         in_specs=[pl.BlockSpec(memory_space=pltpu.SMEM)] + [anywhere] * 4,
-        out_specs=anywhere,
+        out_specs=pl.BlockSpec(memory_space=pltpu.VMEM),
         scratch_shapes=scratch,
         compiler_params=pltpu.CompilerParams(
             collective_id=0, has_side_effects=True, vmem_limit_bytes=56 * 1024 * 1024

time: 45.8 us -> 37.3 us (0.81)
  Pallas kernels: 42.5 us -> 35.8 us
  local copies, waits for them, and re-layouts: 3.13 us -> 1.32 us
    pallas_call x1, Pallas kernels: 42.5 us -> 35.8 us  [body(): pl.pallas_call(functools.partial(kernel, ny, nz, ly, lz, lx, phase_diffus...]
    unnamed x1, local copies, waits for them, and re-layouts: 3.13 us -> 1.32 us
where the time goes in v1:
time: 37.3 us; the launch traced here: 37.2 us
  Pallas kernels  35.8 us (96%)
  local copies, waits for them, and re-layouts  1.32 us (4%)
    pallas_call x1, Pallas kernels, body(): pl.pallas_call(functools.partial(kernel, ny, nz, ly, lz, lx, phase_diffus...  35.8 us
    unnamed x1, local copies, waits for them, and re-layouts  1.32 us

profile of v1, /device:TPU:0, one launch (start us, length us, event | category | flops | bytes accessed | tf_op | source)
XLA Modules:
  0.0 37.2 jit_solution(16066003594257803988)
XLA Ops:
  0.0 35.8 %shard_map.55 = f32[32,64,256]{2,1,0:T(8,128)S(1)} custom-call(f32[4]{0:T(128)} %diff.1, f32[32,64,256]{2,1,0:T(8,128)} %u_hbm.1, f32[32,64,256]{2,1,0:T(8,128)} %s_hbm.1, s32[32,64,256]{2,1,0:T(8,128)} %m_hbm.1, s32[32,64,256]{2,1,0:T(8,128)} %l_hbm.1), custom_call_target="tpu_custom_call" | custom-call | tf_op jit(solution)/shard_map/pallas_call | solution.py:471
  35.8 1.3 %copy.7 = f32[32,64,256]{2,1,0:T(8,128)} copy(f32[32,64,256]{2,1,0:T(8,128)S(1)} %shard_map.55) | data formatting | bytes 4194304

commit v2 on v1

--- a/solution.py
+++ b/solution.py
@@ -67,37 +67,6 @@
 
     greet("gy", me_y, ny)
     greet("gz", me_z, nz)
-    pl.semaphore_wait(barrier, ny + nz - 2)
-
-    halo_y = []
-    for h in range(halves):
-        cols = pl.ds(h * LANES, LANES)
-        for d, (row, place, peer) in enumerate(((ly - 1, 0, up_y), (0, ly + 1, down_y))):
-            copy = pltpu.make_async_remote_copy(
-                src_ref=u_hbm.at[row, :, cols], dst_ref=u_v[h].at[place],
-                send_sem=hy_s.at[h, d], recv_sem=hy_r.at[h, d],
-                device_id={"gy": peer}, device_id_type=MESH,
-            )
-            copy.start()
-            halo_y.append(copy)
-
-    for h in range(halves):
-        loads[1][h].wait()
-        for d, z in ((0, lz - 1), (1, 0)):
-            def pick(y, _):
-                zh_send[d, h, pl.ds(y, 1), :] = u_v[h][y + 1, pl.ds(z, 1), :]
-                return 0
-            lax.fori_loop(0, ly, pick, 0, unroll=8)
-    halo_z = []
-    for d, peer in ((0, up_z), (1, down_z)):
-        copy = pltpu.make_async_remote_copy(
-            src_ref=zh_send.at[d], dst_ref=zh_recv.at[d],
-            send_sem=hz_s.at[d], recv_sem=hz_r.at[d],
-            device_id={"gz": peer}, device_id_type=MESH,
-        )
-        copy.start()
-        halo_z.append(copy)
-
     def spread(axis, me, n, source, target, send, recv, start):
         def one(o, _):
             peer = lax.rem(me + o, n)
@@ -143,12 +112,45 @@
     zones, zzeros = jnp.ones(slab, jnp.float32), jnp.zeros(slab, jnp.float32)
     plane = (lz, LANES)
     ones, zeros = jnp.ones(plane, jnp.float32), jnp.zeros(plane, jnp.float32)
+    pl.semaphore_wait(barrier, ny + nz - 2)
+
+    halo_y = []
+    for h in range(halves):
+        cols = pl.ds(h * LANES, LANES)
+        for d, (row, place, peer) in enumerate(((ly - 1, 0, up_y), (0, ly + 1, down_y))):
+            copy = pltpu.make_async_remote_copy(
+                src_ref=u_hbm.at[row, :, cols], dst_ref=u_v[h].at[place],
+                send_sem=hy_s.at[h, d], recv_sem=hy_r.at[h, d],
+                device_id={"gy": peer}, device_id_type=MESH,
+            )
+            copy.start()
+            halo_y.append(copy)
+
+    for h in range(halves):
+        loads[1][h].wait()
+        for d, z in ((0, lz - 1), (1, 0)):
+            def pick(y, _):
+                zh_send[d, h, pl.ds(y, 1), :] = u_v[h][y + 1, pl.ds(z, 1), :]
+                return 0
+            lax.fori_loop(0, ly, pick, 0, unroll=8)
+    halo_z = []
+    for d, peer in ((0, up_z), (1, down_z)):
+        copy = pltpu.make_async_remote_copy(
+            src_ref=zh_send.at[d], dst_ref=zh_recv.at[d],
+            send_sem=hz_s.at[d], recv_sem=hz_r.at[d],
+            device_id={"gz": peer}, device_id_type=MESH,
+        )
+        copy.start()
+        halo_z.append(copy)
+
     for h in range(halves):
         loads[0][h].wait()
 
-        def matrix_y(y, carry):
-            slack, prod, low, _ = carry
-            at = pl.ds(pl.multiple_of(y * lz, lz), lz)
+    def matrix_y(y, carry):
+        at = pl.ds(pl.multiple_of(y * lz, lz), lz)
+        after = []
+        for h in range(halves):
+            slack, prod, low, _ = carry[h]
             label = l_v[h][y]
             rate = jnp.broadcast_to(inv[0], plane)
             for k in range(1, phases):
@@ -158,9 +160,12 @@
             slack, ratio = eliminate(slack, rate)
             cy[h][at, :] = ratio
             later = prod * ratio
-            return slack, later, low + prod * later, ratio
-
-        _, prod, low, last = lax.fori_loop(0, ly, matrix_y, (ones, ones, zeros, zeros))
+            after.append((slack, later, low + prod * later, ratio))
+        return after
+
+    ends = lax.fori_loop(0, ly, matrix_y, [(ones, ones, zeros, zeros)] * halves)
+    for h in range(halves):
+        _, prod, low, last = ends[h]
         for j in range(ny):
             part = slice(rp * j, rp * (j + 1))
             ye_send[j, h, 0] = low[part]
@@ -174,7 +179,7 @@
             block = g_v[h][pl.ds(pl.multiple_of(b * LANES, LANES), LANES), :]
             cx[pl.ds(h * LANES * pitch_x + b, LANES, stride=pitch_x), :] = block.T
             return 0
-        lax.fori_loop(0, blocks, turn_g, 0, unroll=2)
+        lax.fori_loop(0, blocks, turn_g, 0, unroll=4)
 
     def at_x(i):
         return pl.ds(i * pitch_x, blocks)
@@ -182,16 +187,20 @@
     lines = (blocks, LANES)
     lone, lzero = jnp.ones(lines, jnp.float32), jnp.zeros(lines, jnp.float32)
 
-    def matrix_x(i, carry):
-        one, two = carry
-        one, ratio = eliminate(one, cx[at_x(i), :])
-        cx[at_x(i), :] = ratio
-        two, ratio = eliminate(two, cx[at_x(lx - 1 - i), :])
-        cx[at_x(lx - 1 - i), :] = ratio
-        return one, two
-
-    slack_one, slack_two = lax.fori_loop(0, half_x, matrix_x, (lone, lone), unroll=4)
-    middle = recip(slack_one + slack_two - slack_one * slack_two)
+    steps = half_x // blocks
+
+    def matrix_x(b, carry):
+        slacks = list(carry)
+        places = [[at_x(b * steps + k) for k in range(steps)],
+                  [at_x(lx - 1 - b * steps - k) for k in range(steps)]]
+        rates = [[cx[at, :] for at in side] for side in places]
+        for k in range(steps):
+            for side in range(2):
+                slacks[side], rates[side][k] = eliminate(slacks[side], rates[side][k])
+        for side in range(2):
+            for k in range(steps):
+                cx[places[side][k], :] = rates[side][k]
+        return tuple(slacks)
 
     for copy in halo_y + halo_z:
         copy.wait()
@@ -218,7 +227,8 @@
     sub = lax.broadcasted_iota(jnp.int32, plane, 0)
     lane = lax.broadcasted_iota(jnp.int32, plane, 1)
 
-    def right_x(b, _):
+    def right_x(b, carry):
+        carry = matrix_x(b, carry)
         done = [[] for _ in range(halves)]
         for k in range(per_block):
             y = b * per_block + k
@@ -245,9 +255,10 @@
         for h in range(halves):
             block = jnp.concatenate(done[h], 0)
             rt[pl.ds(h * LANES * pitch_x + b, LANES, stride=pitch_x), :] = block.T
-        return 0
-
-    lax.fori_loop(0, blocks, right_x, 0)
+        return carry
+
+    slack_one, slack_two = lax.fori_loop(0, blocks, right_x, (lone, lone))
+    middle = recip(slack_one + slack_two - slack_one * slack_two)
 
     def forward_x(i, carry):
         one, two = carry
@@ -292,7 +303,7 @@
                 prod = prod * ratio
             return value, prod, head
 
-        value, _, head = lax.fori_loop(0, blocks, local_y, (zeros, ones, zeros))
+        value, _, head = lax.fori_loop(0, blocks, local_y, (zeros, ones, zeros), unroll=2)
         for j in range(ny):
             part = slice(rp * j, rp * (j + 1))
             yp_send[h, j, 0] = head[part]
@@ -330,41 +341,41 @@
 
         lax.fori_loop(0, n, backward, none)
 
-    for h in range(halves):
-        def matrix_z(z, carry):
-            slack, prod, low, _ = carry
-            rate = rz[h][pl.ds(z * pitch_z, ly), :]
-            slack, ratio = eliminate(slack, rate)
+    def matrix_z(z, carry):
+        after = []
+        for h in range(halves):
+            slack, prod, low, _ = carry[h]
+            slack, ratio = eliminate(slack, rz[h][pl.ds(z * pitch_z, ly), :])
             cz[h][z] = ratio
             later = prod * ratio
-            return slack, later, low + prod * later, ratio
-
-        _, prod, low, last = lax.fori_loop(
-            0, lz, matrix_z, (zones, zzeros + 1.0, zzeros, zzeros), unroll=2
-        )
+            after.append((slack, later, low + prod * later, ratio))
+        return after
+
+    state_z = [(zones, zones, zzeros, zzeros)] * halves
+    state_z = lax.fori_loop(0, lz // 2, matrix_z, state_z)
+
+    ye_do(False)
+    for h in range(halves):
+        pivots(ny, lambda k, c: ye_recv[k, h, c], ychain.at[h], (rp, LANES))
+    for h in range(halves):
+        yp_do(h, False)
+
+        def answer_y(k, left, right):
+            ya_send[h, k, 0] = left
+            ya_send[h, k, 1] = right
+
+        chain(ny, lambda k, c: ye_recv[k, h, c], lambda k, c: yp_recv[h, k, c],
+              ychain.at[h], answer_y, (rp, LANES))
+        ya_recv[h, me_y] = ya_send[h, me_y]
+        ya_do(h, True)
+
+    state_z = lax.fori_loop(lz // 2, lz, matrix_z, state_z)
+    for h in range(halves):
+        _, prod, low, last = state_z[h]
         ze[me_z, h, 0] = low
         ze[me_z, h, 1] = prod
         ze[me_z, h, 2] = last
     ze_do(True)
-
-    ye_do(False)
-    for h in range(halves):
-        pivots(ny, lambda k, c: ye_recv[k, h, c], ychain.at[h], (rp, LANES))
-    for h in range(halves):
-        yp_do(h, False)
-
-        def answer_y(k, left, right):
-            ya_send[h, k, 0] = left
-            ya_send[h, k, 1] = right
-
-        chain(ny, lambda k, c: ye_recv[k, h, c], lambda k, c: yp_recv[h, k, c],
-              ychain.at[h], answer_y, (rp, LANES))
-        ya_recv[h, me_y] = ya_send[h, me_y]
-        ya_do(h, True)
-
-    ze_do(False)
-    for h in range(halves):
-        pivots(nz, lambda k, c: ze[k, h, c], zchain.at[h], slab)
 
     for h in range(halves):
         ya_do(h, False)
@@ -377,7 +388,7 @@
             r2[h][at, :] = value
             return value
 
-        lax.fori_loop(0, ly, forward_y, left, unroll=2)
+        lax.fori_loop(0, ly, forward_y, left, unroll=4)
 
         def backward_y(i, value):
             y = ly - 1 - i
@@ -386,7 +397,7 @@
             rz[h][pl.ds(y, lz, stride=pitch_z), :] = g_v[h][at, :] * value - lapz[h][at, :]
             return value
 
-        lax.fori_loop(0, ly, backward_y, right, unroll=2)
+        lax.fori_loop(0, ly, backward_y, right, unroll=4)
 
         def local_z(z, carry):
             value, prod, head = carry
@@ -399,6 +410,9 @@
         zp[h, me_z, 1] = value
         zp_do(h, True)
 
+    ze_do(False)
+    for h in range(halves):
+        pivots(nz, lambda k, c: ze[k, h, c], zchain.at[h], slab)
     for h in range(halves):
         zp_do(h, False)
 

time: 37.3 us -> 35.4 us (0.949)
  Pallas kernels: 35.8 us -> 33.9 us
    pallas_call x1, Pallas kernels: 35.8 us -> 33.9 us  [body(): pl.pallas_call(functools.partial(kernel, ny, nz, ly, lz, lx, phase_diffus...]
where the time goes in v2:
time: 35.4 us; the launch traced here: 35.3 us
  Pallas kernels  33.9 us (96%)
  local copies, waits for them, and re-layouts  1.32 us (4%)
    pallas_call x1, Pallas kernels, body(): pl.pallas_call(functools.partial(kernel, ny, nz, ly, lz, lx, phase_diffus...  33.9 us
    unnamed x1, local copies, waits for them, and re-layouts  1.32 us

profile of v2, /device:TPU:0, one launch (start us, length us, event | category | flops | bytes accessed | tf_op | source)
XLA Modules:
  0.0 35.3 jit_solution(12946069674508750689)
XLA Ops:
  0.0 33.9 %shard_map.55 = f32[32,64,256]{2,1,0:T(8,128)S(1)} custom-call(f32[4]{0:T(128)} %diff.1, f32[32,64,256]{2,1,0:T(8,128)} %u_hbm.1, f32[32,64,256]{2,1,0:T(8,128)} %s_hbm.1, s32[32,64,256]{2,1,0:T(8,128)} %m_hbm.1, s32[32,64,256]{2,1,0:T(8,128)} %l_hbm.1), custom_call_target="tpu_custom_call" | custom-call | tf_op jit(solution)/shard_map/pallas_call | solution.py:485
  33.9 1.3 %copy.7 = f32[32,64,256]{2,1,0:T(8,128)} copy(f32[32,64,256]{2,1,0:T(8,128)S(1)} %shard_map.55) | data formatting | bytes 4194304

commit v3 on v2

--- a/solution.py
+++ b/solution.py
@@ -179,7 +179,7 @@
             block = g_v[h][pl.ds(pl.multiple_of(b * LANES, LANES), LANES), :]
             cx[pl.ds(h * LANES * pitch_x + b, LANES, stride=pitch_x), :] = block.T
             return 0
-        lax.fori_loop(0, blocks, turn_g, 0, unroll=4)
+        lax.fori_loop(0, blocks, turn_g, 0, unroll=8)
 
     def at_x(i):
         return pl.ds(i * pitch_x, blocks)
@@ -257,7 +257,7 @@
             rt[pl.ds(h * LANES * pitch_x + b, LANES, stride=pitch_x), :] = block.T
         return carry
 
-    slack_one, slack_two = lax.fori_loop(0, blocks, right_x, (lone, lone))
+    slack_one, slack_two = lax.fori_loop(0, blocks, right_x, (lone, lone), unroll=2)
     middle = recip(slack_one + slack_two - slack_one * slack_two)
 
     def forward_x(i, carry):
@@ -303,7 +303,7 @@
                 prod = prod * ratio
             return value, prod, head
 
-        value, _, head = lax.fori_loop(0, blocks, local_y, (zeros, ones, zeros), unroll=2)
+        value, _, head = lax.fori_loop(0, blocks, local_y, (zeros, ones, zeros), unroll=4)
         for j in range(ny):
             part = slice(rp * j, rp * (j + 1))
             yp_send[h, j, 0] = head[part]

time: 35.4 us -> 34.1 us (0.963)
  Pallas kernels: 33.9 us -> 32.6 us
    pallas_call x1, Pallas kernels: 33.9 us -> 32.6 us  [body(): pl.pallas_call(functools.partial(kernel, ny, nz, ly, lz, lx, phase_diffus...]
where the time goes in v3:
time: 34.1 us; the launch traced here: 33.9 us
  Pallas kernels  32.6 us (96%)
  local copies, waits for them, and re-layouts  1.32 us (4%)
    pallas_call x1, Pallas kernels, body(): pl.pallas_call(functools.partial(kernel, ny, nz, ly, lz, lx, phase_diffus...  32.6 us
    unnamed x1, local copies, waits for them, and re-layouts  1.32 us

profile of v3, /device:TPU:0, one launch (start us, length us, event | category | flops | bytes accessed | tf_op | source)
XLA Modules:
  0.0 33.9 jit_solution(3199050919053600957)
XLA Ops:
  0.0 32.6 %shard_map.55 = f32[32,64,256]{2,1,0:T(8,128)S(1)} custom-call(f32[4]{0:T(128)} %diff.1, f32[32,64,256]{2,1,0:T(8,128)} %u_hbm.1, f32[32,64,256]{2,1,0:T(8,128)} %s_hbm.1, s32[32,64,256]{2,1,0:T(8,128)} %m_hbm.1, s32[32,64,256]{2,1,0:T(8,128)} %l_hbm.1), custom_call_target="tpu_custom_call" | custom-call | tf_op jit(solution)/shard_map/pallas_call | solution.py:485
  32.6 1.3 %copy.7 = f32[32,64,256]{2,1,0:T(8,128)} copy(f32[32,64,256]{2,1,0:T(8,128)S(1)} %shard_map.55) | data formatting | bytes 4194304
